TPU v7x, 32 devices: a whole 2x2x4 slice. The times are simulated.
32 devices in a mesh: wide: 8 (over z, x), narrow: 4 (over y, core).
Axes of the slice: x: 2, y: 2, z: 4, core: 2. Of those that a mesh axis runs over, the one named last changes fastest.
Arguments:
- activations: bfloat16 [64, 8192], P('wide', 'narrow'), may hold values from -6 to 6
- up_weight: bfloat16 [8192, 28672], P('narrow', 'wide'), may hold values from -0.0625 to 0.0625
- block_mask: int32 [128, 448], P('narrow', 'wide'), may hold values from 0 to 1, as said below
- out_grad: bfloat16 [64, 28672], P('narrow', 'wide'), may hold values from -6 to 6
Outputs:
- output: bfloat16 [64, 28672], P('narrow', 'wide')
- input_grad: bfloat16 [64, 8192], P('wide', 'narrow')
- weight_grad: bfloat16 [8192, 28672], P('narrow', 'wide')
Inputs may be any that keep to these rules, and one draw needn't show every extreme that they name: block_mask holds 0 or 1; the share of kept blocks differs from one block column to another.
All inputs are finite; a program needn't handle non-finite values.
Results may differ from a plain program's by a relative error of at most 0.012.
Values may be sent and summed in bfloat16 or wider, within the bound.
A program may use at most 192 MiB of HBM per device.

v0:
```python
import jax
import jax.numpy as jnp
from jax import lax
from jax.sharding import PartitionSpec as P


def apply_mask(weight, blocks):
    rows_b, cols_b = blocks.shape
    side_rows = weight.shape[0] // rows_b
    side_cols = weight.shape[1] // cols_b
    shaped = weight.reshape(rows_b, side_rows, cols_b, side_cols)
    return (shaped * blocks[:, None, :, None].astype(weight.dtype)).reshape(weight.shape)


def on_device(activations, up_weight, block_mask, out_grad):
    masked = apply_mask(up_weight, block_mask)
    gathered = lax.all_gather(activations, "wide", axis=0, tiled=True)
    partial_sum = jnp.dot(gathered, masked, preferred_element_type=jnp.float32)
    output = lax.psum_scatter(
        partial_sum.astype(jnp.bfloat16), "narrow", scatter_dimension=0, tiled=True
    )
    grad_all = lax.all_gather(out_grad, "narrow", axis=0, tiled=True)
    input_grad = lax.psum_scatter(
        lax.dot_general(
            grad_all, masked, (((1,), (1,)), ((), ())), preferred_element_type=jnp.float32
        ),
        "wide",
        scatter_dimension=0,
        tiled=True,
    ).astype(jnp.bfloat16)
    full_grad = lax.dot_general(
        gathered, grad_all, (((0,), (0,)), ((), ())), preferred_element_type=jnp.float32
    )
    weight_grad = apply_mask(full_grad, block_mask).astype(jnp.bfloat16)
    return (output, input_grad, weight_grad)


def solution(mesh):
    placed = (P("wide", "narrow"), P("narrow", "wide"), P("narrow", "wide"), P("narrow", "wide"))
    return jax.shard_map(
        on_device,
        mesh=mesh,
        in_specs=placed,
        out_specs=(P("narrow", "wide"), P("wide", "narrow"), P("narrow", "wide")),
        check_vma=False,
    )
```

profile of v0, /device:TPU:0, one launch (start us, length us, event | category | flops | bytes accessed | tf_op | source)
XLA Modules:
  0.0 210.2 jit_solution(1157886170441812201)
XLA Ops:
  7.2 0.0 reduce-scatter.5.cloned.1.call-start
  7.2 0.8 fusion.13
  8.0 8.5 %all_gather.7 = bf16[64,3584]{1,0:T(8,128)(2,1)S(1)} all-gather(bf16[16,3584]{1,0:T(8,128)(2,1)} %param.7), channel_id=1, replica_groups=mesh['wide'=8,'narrow'=4] {'narrow'}, dimensions={0}, use_global_device_ids=true | all-gather | bytes 573440 | tf_op jit(solution)/shard_map/all_gather | solution.py:22
  16.5 10.0 %mul.22 = bf16[32,64,56,64]{3,2,1,0:T(8,128)(2,1)} broadcast(bf16[32,56]{1,0:T(8,128)(2,1)S(1)} %get-tuple-element.4), dimensions={0,2} | broadcast | bytes 14683648 | tf_op jit(solution)/shard_map/mul | solution.py:12
  26.5 36.1 %mul.23 = bf16[2048,3584]{1,0:T(8,128)(2,1)} reshape(bf16[32,64,56,64]{3,2,1,0:T(8,128)(2,1)} %mul.22) | data formatting | bytes 29360128 | tf_op jit(solution)/shard_map/mul | solution.py:12
  62.6 0.0 copy-start
  62.6 12.6 %fusion.10 = f32[64,2048]{1,0:T(8,128)} fusion(bf16[64,3584]{1,0:T(8,128)(2,1)S(1)} %all_gather.7, bf16[2048,3584]{1,0:T(8,128)(2,1)} %param.5, bf16[2048,3584]{1,0:T(8,128)(2,1)} %mul.23), kind=kOutput, calls=%fused_computation.7 | convolution fusion | flops 946864128 | bytes 30343168 | tf_op jit(solution)/shard_map/dot_general | solution.py:24
  75.2 0.0 reduce-scatter.5.cloned.1.call-update
  75.2 0.0 reduce-scatter.3.cloned.1.call-start
  75.3 0.0 copy-done
  75.3 31.4 %all_gather.6 = bf16[64,2048]{1,0:T(8,128)(2,1)S(1)} all-gather(bf16[8,2048]{1,0:T(8,128)(2,1)S(1)} %copy-done), channel_id=1, replica_groups=mesh['wide'=8,'narrow'=4] {'wide'}, dimensions={0}, use_global_device_ids=true | all-gather | bytes 294912 | tf_op jit(solution)/shard_map/all_gather | solution.py:17
  106.7 13.0 %fusion.7 = bf16[64,3584]{1,0:T(8,128)(2,1)} fusion(bf16[64,2048]{1,0:T(8,128)(2,1)S(1)} %all_gather.6, bf16[2048,3584]{1,0:T(8,128)(2,1)} %param.5, bf16[2048,3584]{1,0:T(8,128)(2,1)} %mul.23), kind=kOutput, calls=%fused_computation.6 | convolution fusion | flops 947093504 | bytes 30081024 | tf_op jit(solution)/shard_map/dot_general | solution.py:18
  119.7 0.0 reduce-scatter.3.cloned.1.call-update
  119.8 19.0 %mul.25 = f32[32,64,56,64]{3,2,1,0:T(8,128)} broadcast(f32[32,56]{1,0:T(8,128)S(1)} %get-tuple-element.3), dimensions={0,2} | broadcast | bytes 29367296 | tf_op jit(solution)/shard_map/mul | solution.py:12
  138.8 45.9 %mul.26 = f32[2048,3584]{1,0:T(8,128)} reshape(f32[32,64,56,64]{3,2,1,0:T(8,128)} %mul.25) | data formatting | bytes 58720256 | tf_op jit(solution)/shard_map/mul | solution.py:12
  184.7 17.1 %multiply_convert_fusion = bf16[2048,3584]{1,0:T(8,128)(2,1)} fusion(f32[2048,3584]{1,0:T(8,128)} %mul.26, bf16[64,2048]{1,0:T(8,128)(2,1)S(1)} %all_gather.6, bf16[64,3584]{1,0:T(8,128)(2,1)S(1)} %all_gather.7), kind=kOutput, calls=%fused_computation | convolution fusion | flops 954204160 | bytes 44761088 | tf_op jit(solution)/shard_map/dot_general | solution.py:31
  201.9 0.0 reduce-scatter.5.cloned.1.call-done
  201.9 1.5 convert_element_type.23
  203.3 0.0 reduce-scatter.3.cloned.1.call-done
Async XLA Ops:
  7.2 194.7 %reduce-scatter.5.cloned.1.call-start = ((), (), s32[]{:S(2)}) async-start(), calls=%async_computation.3 | async-start | bytes 589824 | tf_op jit(solution)/shard_map/reduce_scatter | solution.py:23
  62.6 12.7 %copy-start = (bf16[8,2048]{1,0:T(8,128)(2,1)S(1)}, bf16[8,2048]{1,0:T(8,128)(2,1)}, u32[]{:S(2)}) copy-start(bf16[8,2048]{1,0:T(8,128)(2,1)} %param.4) | copy-start | bytes 98308
  75.2 128.1 %reduce-scatter.3.cloned.1.call-start = ((), (), s32[]{:S(2)}) async-start(), calls=%async_computation.2 | async-start | bytes 573440 | tf_op jit(solution)/shard_map/reduce_scatter | solution.py:19
Sparse Core Ops, SparseCore 0:
  75.3 62.7 reduce-scatter.4
  141.4 20.1 reduce-scatter.2
where the time goes:
time: 212 us; the launch traced here: 210 us
  local copies, waits for them, and re-layouts  111 us (52%)
  matrix products  42.7 us (20%)
  blocking collectives  39.9 us (19%)
  between operations  14 us (7%)
  other arithmetic  2.26 us (1%)
    mul x4, local copies, waits for them, and re-layouts, apply_mask(): shaped * blocks[:, None, :, None].astype(weight.dtype)  111 us
    all_gather x1, blocking collectives, on_device(): gathered = lax.all_gather(activations, 'wide', axis=0, tiled=True)  31.4 us
    dot_general x1, matrix products, on_device(): lax.dot_general(gathered, grad_all, (((0,), (0,)), ((), ())), preferred_e...  17.1 us
    dot_general x1, matrix products, on_device(): partial_sum = jnp.dot(gathered, masked, preferred_element_type=jnp.float32)  13 us
    dot_general x1, matrix products, on_device(): lax.dot_general(grad_all, masked, (((1,), (1,)), ((), ())), preferred_ele...  12.6 us
    all_gather x1, blocking collectives, on_device(): grad_all = lax.all_gather(out_grad, 'narrow', axis=0, tiled=True)  8.49 us
  transfers between devices with their start and end apart: 2, of which 0 were waited for; matrix products, arithmetic and copies ran while one was open for 46% of the time, Pallas kernels for 0%

commit v1 on v0

v1 whole, which is shorter than its diff:
```python
import functools

import jax
import jax.numpy as jnp
from jax import lax
from jax.experimental import pallas as pl
from jax.experimental.pallas import tpu as pltpu
from jax.sharding import PartitionSpec as P

MESH = pl.DeviceIdType.MESH
BF16 = jnp.bfloat16
F32 = jnp.float32
ROWS = 256


def column_chunk(cols):
    return 512 if cols % 512 == 0 else cols


def exchange_kernel(
    nw, nn, side,
    act_ref, w_hbm, mask_ref, og_ref,
    out_ref, ig_ref, act_out, og_out, mask_out,
    w, act_all, og_all, ig_part, ig_recv, out_part, out_recv,
    w_sem, act_send, act_recv, og_send, og_recv, ig_send, ig_rsem, out_send, out_rsem,
):
    iw = lax.axis_index("wide")
    jn = lax.axis_index("narrow")
    rows, cols = w_hbm.shape
    steps = rows // ROWS
    blocks = ROWS // side
    tokens = nw * act_ref.shape[0]

    def fetch(c):
        at = pl.ds(pl.multiple_of(c * ROWS, ROWS), ROWS)
        return pltpu.make_async_copy(w_hbm.at[at], w.at[at], w_sem.at[c])

    for c in range(steps):
        fetch(c).start()

    barrier = pltpu.get_barrier_semaphore()
    for off in range(1, nw):
        pl.semaphore_signal(
            barrier, inc=1, device_id={"wide": lax.rem(iw + off, nw)}, device_id_type=MESH
        )
    for off in range(1, nn):
        pl.semaphore_signal(
            barrier, inc=1, device_id={"narrow": lax.rem(jn + off, nn)}, device_id_type=MESH
        )

    at_col = lax.broadcasted_iota(jnp.int32, (cols // side, cols), 1)
    at_row = lax.broadcasted_iota(jnp.int32, (cols // side, cols), 0)
    low = at_row * side
    spread = jnp.where((at_col >= low) & (at_col < low + side), 1.0, 0.0).astype(BF16)
    mask_out[...] = jnp.dot(
        mask_ref[...].astype(F32).astype(BF16), spread, preferred_element_type=F32
    )
    act_all[iw] = act_ref[...]
    og_all[jn] = og_ref[...]

    pl.semaphore_wait(barrier, nw + nn - 2)

    def wide_copy(src, dst, send, recv, off):
        return pltpu.make_async_remote_copy(
            src_ref=src, dst_ref=dst, send_sem=send.at[off], recv_sem=recv.at[off],
            device_id={"wide": lax.rem(iw + off, nw)}, device_id_type=MESH,
        )

    def narrow_copy(src, dst, send, recv, off):
        return pltpu.make_async_remote_copy(
            src_ref=src, dst_ref=dst, send_sem=send.at[off], recv_sem=recv.at[off],
            device_id={"narrow": lax.rem(jn + off, nn)}, device_id_type=MESH,
        )

    og_copies = [
        narrow_copy(og_ref, og_all.at[jn], og_send, og_recv, off) for off in range(1, nn)
    ]
    act_copies = [
        wide_copy(act_ref, act_all.at[iw], act_send, act_recv, off) for off in range(1, nw)
    ]
    for copy in og_copies + act_copies:
        copy.start()

    @pl.loop(0, steps)
    def _(c):
        fetch(c).wait()
        for b in range(blocks):
            kept = mask_out[pl.ds(c * blocks + b, 1), :].astype(BF16)
            at = pl.ds(pl.multiple_of(c * ROWS + b * side, side), side)
            w[at, :] = w[at, :] * kept

    for copy in og_copies:
        copy.wait()
    og_out[...] = og_all[...].reshape(tokens, cols)

    @pl.loop(0, steps)
    def _(c):
        at = pl.ds(pl.multiple_of(c * ROWS, ROWS), ROWS)
        part = lax.dot_general(
            og_out[...], w[at, :], (((1,), (1,)), ((), ())), preferred_element_type=F32
        )
        ig_part[:, :, at] = part.reshape(nw, tokens // nw, ROWS).astype(BF16)

    ig_copies = [
        wide_copy(
            ig_part.at[lax.rem(iw + off, nw)], ig_recv.at[off], ig_send, ig_rsem, off
        )
        for off in range(1, nw)
    ]
    for copy in ig_copies:
        copy.start()

    for copy in act_copies:
        copy.wait()
    act_out[...] = act_all[...].astype(F32).reshape(tokens, rows).astype(BF16)

    wide_cols = column_chunk(cols)

    @pl.loop(0, cols // wide_cols)
    def _(c):
        at = pl.ds(pl.multiple_of(c * wide_cols, 128) if wide_cols < cols else 0, wide_cols)
        part = jnp.dot(act_out[...], w[:, at], preferred_element_type=F32)
        out_part[:, :, at] = part.astype(BF16).reshape(nn, tokens // nn, wide_cols)

    out_copies = [
        narrow_copy(
            out_part.at[lax.rem(jn + off, nn)], out_recv.at[off], out_send, out_rsem, off
        )
        for off in range(1, nn)
    ]
    for copy in out_copies:
        copy.start()

    for copy in ig_copies:
        copy.wait()
    total = ig_part[iw].astype(F32)
    for off in range(1, nw):
        total = total + ig_recv[off].astype(F32)
    ig_ref[...] = total.astype(BF16)

    for copy in out_copies:
        copy.wait()
    total = out_part[jn].astype(F32)
    for off in range(1, nn):
        total = total + out_recv[off].astype(F32)
    out_ref[...] = total.astype(BF16)


def weight_kernel(side, act_ref, og_ref, mask_ref, grad_ref):
    step = pl.program_id(0)
    high, cols = grad_ref.shape
    blocks = high // side
    chunk = column_chunk(cols)
    turned = act_ref[...].T

    for c in range(cols // chunk):
        at = slice(c * chunk, (c + 1) * chunk)
        grad = jnp.dot(turned, og_ref[:, at], preferred_element_type=F32).astype(BF16)
        for b in range(blocks):
            kept = mask_ref[pl.ds(step * blocks + b, 1), at].astype(BF16)
            grad_ref[b * side:(b + 1) * side, at] = grad[b * side:(b + 1) * side] * kept


def on_device(nw, nn, activations, up_weight, block_mask, out_grad):
    rows, cols = up_weight.shape
    own_w, own_n = activations.shape[0], out_grad.shape[0]
    tokens = nw * own_w
    side = rows // block_mask.shape[0]
    vmem = pl.BlockSpec(memory_space=pltpu.VMEM)
    dma = pltpu.SemaphoreType.DMA
    output, input_grad, act_all, og_all, mask_wide = pl.pallas_call(
        functools.partial(exchange_kernel, nw, nn, side),
        out_shape=(
            jax.ShapeDtypeStruct((own_n, cols), BF16),
            jax.ShapeDtypeStruct((own_w, rows), BF16),
            jax.ShapeDtypeStruct((tokens, rows), BF16),
            jax.ShapeDtypeStruct((tokens, cols), BF16),
            jax.ShapeDtypeStruct((block_mask.shape[0], cols), F32),
        ),
        in_specs=[vmem, pl.BlockSpec(memory_space=pl.ANY), vmem, vmem],
        out_specs=(vmem,) * 5,
        scratch_shapes=[
            pltpu.VMEM((rows, cols), BF16),
            pltpu.VMEM((nw, own_w, rows), BF16),
            pltpu.VMEM((nn, own_n, cols), BF16),
            pltpu.VMEM((nw, own_w, rows), BF16),
            pltpu.VMEM((nw, own_w, rows), BF16),
            pltpu.VMEM((nn, own_n, cols), BF16),
            pltpu.VMEM((nn, own_n, cols), BF16),
            dma((rows // ROWS,)),
            dma((nw,)), dma((nw,)),
            dma((nn,)), dma((nn,)),
            dma((nw,)), dma((nw,)),
            dma((nn,)), dma((nn,)),
        ],
        compiler_params=pltpu.CompilerParams(
            collective_id=0, has_side_effects=True, vmem_limit_bytes=48 * 2**20
        ),
        cost_estimate=pl.CostEstimate(
            flops=4 * tokens * rows * cols, bytes_accessed=2 * rows * cols, transcendentals=0
        ),
        name="exchange",
    )(activations, up_weight, block_mask, out_grad)
    weight_grad = pl.pallas_call(
        functools.partial(weight_kernel, side),
        grid=(rows // ROWS,),
        out_shape=jax.ShapeDtypeStruct((rows, cols), BF16),
        in_specs=[
            pl.BlockSpec((tokens, ROWS), lambda i: (0, i)),
            pl.BlockSpec((tokens, cols), lambda i: (0, 0)),
            pl.BlockSpec(mask_wide.shape, lambda i: (0, 0)),
        ],
        out_specs=pl.BlockSpec((ROWS, cols), lambda i: (i, 0)),
        compiler_params=pltpu.CompilerParams(vmem_limit_bytes=32 * 2**20),
        cost_estimate=pl.CostEstimate(
            flops=2 * tokens * rows * cols, bytes_accessed=2 * rows * cols, transcendentals=0
        ),
        name="weight_grad",
    )(act_all, og_all, mask_wide)
    return (output, input_grad, weight_grad)


def solution(mesh):
    placed = (P("wide", "narrow"), P("narrow", "wide"), P("narrow", "wide"), P("narrow", "wide"))
    return jax.shard_map(
        functools.partial(on_device, mesh.shape["wide"], mesh.shape["narrow"]),
        mesh=mesh,
        in_specs=placed,
        out_specs=(P("narrow", "wide"), P("wide", "narrow"), P("narrow", "wide")),
        check_vma=False,
    )
```

time: 212 us -> 40.4 us (0.19)
  the two profiles are of different devices: /device:TPU:0 before, /device:TPU:1 now
where the time goes in v1:
time: 40.4 us; the launch traced here: 40.1 us
  Pallas kernels  35.9 us (89%)
  local copies, waits for them, and re-layouts  3.63 us (9%)
  between operations  0.65 us (2%)
    pallas_call x1, Pallas kernels, on_device(): pl.pallas_call(functools.partial(exchange_kernel, nw, nn, side), out_shap...  27.6 us
    pallas_call x1, Pallas kernels, on_device(): pl.pallas_call(functools.partial(weight_kernel, side), grid=(rows // ROWS...  8.29 us
    unnamed x8, local copies, waits for them, and re-layouts  3.63 us

profile of v1, /device:TPU:1, one launch (start us, length us, event | category | flops | bytes accessed | tf_op | source)
XLA Modules:
  0.0 40.1 jit_solution(13904950169114075742)
XLA Ops:
  0.6 0.0 copy-start
  0.6 0.9 %copy-done = bf16[16,3584]{1,0:T(8,128)(2,1)S(1)} copy-done((bf16[16,3584]{1,0:T(8,128)(2,1)S(1)}, bf16[16,3584]{1,0:T(8,128)(2,1)}, u32[]{:S(2)}) %copy-start) | copy-done | bytes 114712
  1.5 0.0 copy-start.1
  1.5 0.8 %copy-done.1 = bf16[8,2048]{1,0:T(8,128)(2,1)S(1)} copy-done((bf16[8,2048]{1,0:T(8,128)(2,1)S(1)}, bf16[8,2048]{1,0:T(8,128)(2,1)}, u32[]{:S(2)}) %copy-start.1) | copy-done | bytes 32792
  2.3 0.0 copy-start.2
  2.3 0.7 %copy-done.2 = s32[32,56]{1,0:T(8,128)S(1)} copy-done((s32[32,56]{1,0:T(8,128)S(1)}, s32[32,56]{1,0:T(8,128)}, u32[]{:S(2)}) %copy-start.2) | copy-done | bytes 7192
  3.0 27.6 %exchange.1 = (bf16[16,3584]{1,0:T(8,128)(2,1)S(1)}, bf16[8,2048]{1,0:T(8,128)(2,1)S(1)}, bf16[64,2048]{1,0:T(8,128)(2,1)S(1)}, bf16[64,3584]{1,0:T(8,128)(2,1)S(1)}, f32[32,3584]{1,0:T(8,128)S(1)}) custom-call(bf16[8,2048]{1,0:T(8,128)(2,1)S(1)} %copy-done.1, bf16[2048,3584]{1,0:T(8,128)(2,1)} %w_hbm.1, s32[32,56]{1,0:T(8,128)S(1)} %copy-done.2, ...), custom_call_target="tpu_custom_call" | custom-call | flops 1879048192 | bytes 14680064 | tf_op jit(solution)/shard_map/exchange/pallas_call | solution.py:171
  30.6 8.3 %weight_grad.1 = bf16[2048,3584]{1,0:T(8,128)(2,1)} custom-call(bf16[64,2048]{1,0:T(8,128)(2,1)S(1)} %get-tuple-element.10.act_ref, bf16[64,3584]{1,0:T(8,128)(2,1)S(1)} %get-tuple-element.11.og_ref, f32[32,3584]{1,0:T(8,128)S(1)} %get-tuple-element.12.mask_ref), custom_call_target="tpu_custom_call" | custom-call | flops 939524096 | bytes 14680064 | tf_op jit(solution)/shard_map/weight_grad/pallas_call | solution.py:204
  38.9 0.6 %copy.9 = bf16[16,3584]{1,0:T(8,128)(2,1)} copy(bf16[16,3584]{1,0:T(8,128)(2,1)S(1)} %get-tuple-element.16) | data formatting | bytes 229376
  39.5 0.6 %copy.10 = bf16[8,2048]{1,0:T(8,128)(2,1)} copy(bf16[8,2048]{1,0:T(8,128)(2,1)S(1)} %get-tuple-element.17) | data formatting | bytes 65536
Async XLA Ops:
  0.6 0.9 %copy-start = (bf16[16,3584]{1,0:T(8,128)(2,1)S(1)}, bf16[16,3584]{1,0:T(8,128)(2,1)}, u32[]{:S(2)}) copy-start(bf16[16,3584]{1,0:T(8,128)(2,1)} %og_ref.1) | copy-start | bytes 344068
  1.5 0.8 %copy-start.1 = (bf16[8,2048]{1,0:T(8,128)(2,1)S(1)}, bf16[8,2048]{1,0:T(8,128)(2,1)}, u32[]{:S(2)}) copy-start(bf16[8,2048]{1,0:T(8,128)(2,1)} %act_ref.1) | copy-start | bytes 98308
  2.3 0.7 %copy-start.2 = (s32[32,56]{1,0:T(8,128)S(1)}, s32[32,56]{1,0:T(8,128)}, u32[]{:S(2)}) copy-start(s32[32,56]{1,0:T(8,128)} %mask_ref.1) | copy-start | bytes 21508

commit v2 on v1

v2 whole, which is shorter than its diff:
```python
import functools

import jax
import jax.numpy as jnp
from jax import lax
from jax.experimental import pallas as pl
from jax.experimental.pallas import tpu as pltpu
from jax.sharding import PartitionSpec as P

MESH = pl.DeviceIdType.MESH
BF16 = jnp.bfloat16
F32 = jnp.float32
ROWS = 256


def column_chunk(cols):
    return 512 if cols % 512 == 0 else cols


def halves(count):
    middle = (count + 1) // 2
    return ((0, middle), (middle, count)) if count > 1 else ((0, count),)


def grad_rows(side, act_ref, og_ref, mask_ref, first, grad_ref, at):
    cols = og_ref.shape[1]
    tile_cols = 256 if cols % 256 == 0 else cols
    tile_rows = 2 * side
    turned = act_ref[:, pl.ds(first, ROWS)].T
    for r in range(ROWS // tile_rows):
        left = turned[r * tile_rows:(r + 1) * tile_rows]
        for c in range(cols // tile_cols):
            across = slice(c * tile_cols, (c + 1) * tile_cols)
            grad = jnp.dot(left, og_ref[:, across], preferred_element_type=F32).astype(BF16)
            for b in range(tile_rows // side):
                row = r * tile_rows + b * side
                kept = mask_ref[pl.ds((first + row) // side, 1), across].astype(BF16)
                grad_ref[pl.ds(at + row, side), across] = grad[b * side:(b + 1) * side] * kept


def exchange_kernel(
    nw, nn, side,
    act_hbm, w_hbm, mask_hbm, og_hbm,
    out_ref, ig_ref, act_out, og_out, mask_out, grad_out,
    w, mask, act_all, og_all, ig_part, ig_recv, out_part, out_recv,
    in_sem, w_sem, act_send, act_recv, og_send, og_recv,
    ig_send, ig_rsem, out_send, out_rsem,
):
    iw = lax.axis_index("wide")
    jn = lax.axis_index("narrow")
    rows, cols = w_hbm.shape
    steps = rows // ROWS
    blocks = ROWS // side
    tokens = nw * act_hbm.shape[0]

    def fetch(c):
        at = pl.ds(pl.multiple_of(c * ROWS, ROWS), ROWS)
        return pltpu.make_async_copy(w_hbm.at[at], w.at[at], w_sem.at[c])

    barrier = pltpu.get_barrier_semaphore()
    for off in range(1, nw):
        pl.semaphore_signal(
            barrier, inc=1, device_id={"wide": lax.rem(iw + off, nw)}, device_id_type=MESH
        )
    for off in range(1, nn):
        pl.semaphore_signal(
            barrier, inc=1, device_id={"narrow": lax.rem(jn + off, nn)}, device_id_type=MESH
        )
    own_copies = [
        pltpu.make_async_copy(mask_hbm, mask, in_sem.at[0]),
        pltpu.make_async_copy(act_hbm, act_all.at[iw], in_sem.at[1]),
        pltpu.make_async_copy(og_hbm, og_all.at[jn], in_sem.at[2]),
    ]
    for copy in own_copies:
        copy.start()
    for c in range(steps):
        fetch(c).start()

    at_col = lax.broadcasted_iota(jnp.int32, (cols // side, cols), 1)
    low = lax.broadcasted_iota(jnp.int32, (cols // side, cols), 0) * side
    spread = jnp.where((at_col >= low) & (at_col < low + side), 1.0, 0.0).astype(BF16)
    own_copies[0].wait()
    mask_out[...] = jnp.dot(
        mask[...].astype(F32).astype(BF16), spread, preferred_element_type=F32
    )

    pl.semaphore_wait(barrier, nw + nn - 2)

    def wide_copy(src, dst, send, recv, off):
        return pltpu.make_async_remote_copy(
            src_ref=src, dst_ref=dst, send_sem=send, recv_sem=recv,
            device_id={"wide": lax.rem(iw + off, nw)}, device_id_type=MESH,
        )

    def narrow_copy(src, dst, send, recv, to):
        return pltpu.make_async_remote_copy(
            src_ref=src, dst_ref=dst, send_sem=send, recv_sem=recv,
            device_id={"narrow": to}, device_id_type=MESH,
        )

    pair, place = jn // 2, jn % 2
    mate = pair * 2 + (1 - place)
    across = [lax.rem(pair + off, nn // 2) * 2 + place for off in range(nn // 2)]
    origin = [lax.rem(pair + nn // 2 - off, nn // 2) * 2 + place for off in range(nn // 2)]
    far = [
        narrow_copy(og_hbm, og_all.at[jn], og_send.at[off], og_recv.at[off], across[off])
        for off in range(1, nn // 2)
    ]
    near = [
        narrow_copy(
            og_hbm if off == 0 else og_all.at[origin[off]], og_all.at[origin[off]],
            og_send.at[nn // 2 + off], og_recv.at[nn // 2 + off], mate,
        )
        for off in range(nn // 2)
    ]
    act_copies = [
        wide_copy(act_hbm, act_all.at[iw], act_send.at[off], act_recv.at[off], off)
        for off in range(1, nw)
    ]
    for copy in far + near[:1] + act_copies:
        copy.start()

    def mask_rows(c):
        fetch(c).wait()
        for b in range(blocks):
            kept = mask_out[pl.ds(c * blocks + b, 1), :].astype(BF16)
            at = pl.ds(pl.multiple_of(c * ROWS + b * side, side), side)
            w[at, :] = w[at, :] * kept

    pl.loop(0, steps // 2)(mask_rows)
    for arrived, passed in zip(far, near[1:]):
        arrived.wait_recv()
        passed.start()
    pl.loop(steps // 2, steps)(mask_rows)

    for copy in far:
        copy.wait_send()
    for copy in near:
        copy.wait()
    for copy in own_copies[1:]:
        copy.wait()
    og_out[...] = og_all[...].reshape(tokens, cols)

    ig_copies = []
    for part, (start, stop) in enumerate(halves(steps)):

        @pl.loop(start, stop)
        def _(c):
            at = pl.ds(pl.multiple_of(c * ROWS, ROWS), ROWS)
            term = lax.dot_general(
                og_out[...], w[at, :], (((1,), (1,)), ((), ())), preferred_element_type=F32
            )
            ig_part[:, :, at] = term.reshape(nw, tokens // nw, ROWS).astype(BF16)

        at = pl.ds(start * ROWS, (stop - start) * ROWS)
        for off in range(1, nw):
            copy = wide_copy(
                ig_part.at[lax.rem(iw + off, nw), :, at], ig_recv.at[off, :, at],
                ig_send.at[part, off], ig_rsem.at[part, off], off,
            )
            copy.start()
            ig_copies.append(copy)

    for copy in act_copies:
        copy.wait()
    act_out[...] = act_all[...].astype(F32).reshape(tokens, rows).astype(BF16)

    wide_cols = column_chunk(cols)
    out_copies = []
    for part, (start, stop) in enumerate(halves(cols // wide_cols)):

        @pl.loop(start, stop)
        def _(c):
            at = pl.ds(pl.multiple_of(c * wide_cols, 128) if wide_cols < cols else 0, wide_cols)
            term = jnp.dot(act_out[...], w[:, at], preferred_element_type=F32)
            out_part[:, :, at] = term.astype(BF16).reshape(nn, tokens // nn, wide_cols)

        at = pl.ds(start * wide_cols, (stop - start) * wide_cols)
        for off in range(1, nn):
            to = lax.rem(jn + off, nn)
            copy = narrow_copy(
                out_part.at[to, :, at], out_recv.at[off, :, at],
                out_send.at[part, off], out_rsem.at[part, off], to,
            )
            copy.start()
            out_copies.append(copy)

    @pl.loop(0, grad_out.shape[0] // ROWS)
    def _(c):
        at = pl.multiple_of(c * ROWS, ROWS)
        grad_rows(side, act_out, og_out, mask_out, at, grad_out, at)

    for copy in ig_copies:
        copy.wait()
    total = ig_part[iw].astype(F32)
    for off in range(1, nw):
        total = total + ig_recv[off].astype(F32)
    ig_ref[...] = total.astype(BF16)

    for copy in out_copies:
        copy.wait()
    total = out_part[jn].astype(F32)
    for off in range(1, nn):
        total = total + out_recv[off].astype(F32)
    out_ref[...] = total.astype(BF16)


def weight_kernel(
    side, act_ref, og_ref, mask_ref, early_ref, out_in, ig_in,
    out_hbm, ig_hbm, grad_hbm, late, sems, late_sems,
):
    early = early_ref.shape[0]
    copies = [
        pltpu.make_async_copy(early_ref, grad_hbm.at[pl.ds(0, early)], sems.at[0]),
        pltpu.make_async_copy(out_in, out_hbm, sems.at[1]),
        pltpu.make_async_copy(ig_in, ig_hbm, sems.at[2]),
    ]
    for copy in copies:
        copy.start()

    def written(c):
        at = pl.multiple_of(c * ROWS, ROWS)
        return pltpu.make_async_copy(
            late.at[pl.ds(at, ROWS)], grad_hbm.at[pl.ds(early + at, ROWS)], late_sems.at[c]
        )

    count = late.shape[0] // ROWS

    @pl.loop(0, count)
    def _(c):
        at = pl.multiple_of(c * ROWS, ROWS)
        grad_rows(side, act_ref, og_ref, mask_ref, early + at, late, at)
        written(c).start()

    for copy in copies:
        copy.wait()
    for c in range(count):
        written(c).wait()


def on_device(nw, nn, activations, up_weight, block_mask, out_grad):
    rows, cols = up_weight.shape
    own_w, own_n = activations.shape[0], out_grad.shape[0]
    tokens = nw * own_w
    side = rows // block_mask.shape[0]
    early = rows // ROWS // 2 * ROWS
    vmem = pl.BlockSpec(memory_space=pltpu.VMEM)
    hbm = pl.BlockSpec(memory_space=pltpu.HBM)
    dma = pltpu.SemaphoreType.DMA
    shape = jax.ShapeDtypeStruct
    output, input_grad, act_all, og_all, mask_wide, grad_early = pl.pallas_call(
        functools.partial(exchange_kernel, nw, nn, side),
        out_shape=(
            shape((own_n, cols), BF16),
            shape((own_w, rows), BF16),
            shape((tokens, rows), BF16),
            shape((tokens, cols), BF16),
            shape((block_mask.shape[0], cols), F32),
            shape((early, cols), BF16),
        ),
        in_specs=[hbm] * 4,
        out_specs=(vmem,) * 6,
        scratch_shapes=[
            pltpu.VMEM((rows, cols), BF16),
            pltpu.VMEM(block_mask.shape, block_mask.dtype),
            pltpu.VMEM((nw, own_w, rows), BF16),
            pltpu.VMEM((nn, own_n, cols), BF16),
            pltpu.VMEM((nw, own_w, rows), BF16),
            pltpu.VMEM((nw, own_w, rows), BF16),
            pltpu.VMEM((nn, own_n, cols), BF16),
            pltpu.VMEM((nn, own_n, cols), BF16),
            dma((3,)),
            dma((rows // ROWS,)),
            dma((nw,)), dma((nw,)),
            dma((nn,)), dma((nn,)),
            dma((2, nw)), dma((2, nw)),
            dma((2, nn)), dma((2, nn)),
        ],
        compiler_params=pltpu.CompilerParams(
            collective_id=0, has_side_effects=True, vmem_limit_bytes=36 * 2**20
        ),
        cost_estimate=pl.CostEstimate(
            flops=4 * tokens * rows * cols, bytes_accessed=2 * rows * cols, transcendentals=0
        ),
        name="exchange",
    )(activations, up_weight, block_mask, out_grad)
    output, input_grad, weight_grad = pl.pallas_call(
        functools.partial(weight_kernel, side),
        out_shape=(
            shape((own_n, cols), BF16),
            shape((own_w, rows), BF16),
            shape((rows, cols), BF16),
        ),
        in_specs=[vmem] * 6,
        out_specs=(hbm,) * 3,
        scratch_shapes=[
            pltpu.VMEM((rows - early, cols), BF16),
            dma((3,)),
            dma(((rows - early) // ROWS,)),
        ],
        compiler_params=pltpu.CompilerParams(vmem_limit_bytes=28 * 2**20),
        cost_estimate=pl.CostEstimate(
            flops=2 * tokens * rows * cols, bytes_accessed=2 * rows * cols, transcendentals=0
        ),
        name="weight_grad",
    )(act_all, og_all, mask_wide, grad_early, output, input_grad)
    return (output, input_grad, weight_grad)


def solution(mesh):
    placed = (P("wide", "narrow"), P("narrow", "wide"), P("narrow", "wide"), P("narrow", "wide"))
    return jax.shard_map(
        functools.partial(on_device, mesh.shape["wide"], mesh.shape["narrow"]),
        mesh=mesh,
        in_specs=placed,
        out_specs=(P("narrow", "wide"), P("wide", "narrow"), P("narrow", "wide")),
        check_vma=False,
    )
```

time: 40.4 us -> 34.2 us (0.85)
  Pallas kernels: 35.9 us -> 31 us
  local copies, waits for them, and re-layouts: 3.63 us -> 2.37 us
    pallas_call x1, Pallas kernels: 8.29 us -> 5.41 us  [on_device(): pl.pallas_call(functools.partial(weight_kernel, side), out_shape=(shape((...]
    pallas_call x1, Pallas kernels: 27.6 us -> 25.6 us  [on_device(): pl.pallas_call(functools.partial(exchange_kernel, nw, nn, side), out_shap...]
    unnamed x8 -> x6, local copies, waits for them, and re-layouts: 3.63 us -> 2.37 us
where the time goes in v2:
time: 34.2 us; the launch traced here: 34 us
  Pallas kernels  31 us (91%)
  local copies, waits for them, and re-layouts  2.37 us (7%)
  between operations  0.65 us (2%)
    pallas_call x1, Pallas kernels, on_device(): pl.pallas_call(functools.partial(exchange_kernel, nw, nn, side), out_shap...  25.6 us
    pallas_call x1, Pallas kernels, on_device(): pl.pallas_call(functools.partial(weight_kernel, side), out_shape=(shape((...  5.41 us
    unnamed x6, local copies, waits for them, and re-layouts  2.37 us

profile of v2, /device:TPU:1, one launch (start us, length us, event | category | flops | bytes accessed | tf_op | source)
XLA Modules:
  0.0 34.0 jit_solution(9286521764445961225)
XLA Ops:
  0.6 0.0 copy-start
  0.6 0.9 %copy-done = bf16[16,3584]{1,0:T(8,128)(2,1)S(1)} copy-done((bf16[16,3584]{1,0:T(8,128)(2,1)S(1)}, bf16[16,3584]{1,0:T(8,128)(2,1)}, u32[]{:S(2)}) %copy-start) | copy-done | bytes 114712
  1.5 0.0 copy-start.1
  1.5 0.8 %copy-done.1 = bf16[8,2048]{1,0:T(8,128)(2,1)S(1)} copy-done((bf16[8,2048]{1,0:T(8,128)(2,1)S(1)}, bf16[8,2048]{1,0:T(8,128)(2,1)}, u32[]{:S(2)}) %copy-start.1) | copy-done | bytes 32792
  2.3 0.0 copy-start.2
  2.3 0.7 %copy-done.2 = s32[32,56]{1,0:T(8,128)S(1)} copy-done((s32[32,56]{1,0:T(8,128)S(1)}, s32[32,56]{1,0:T(8,128)}, u32[]{:S(2)}) %copy-start.2) | copy-done | bytes 7192
  3.0 25.6 %exchange.1 = (bf16[16,3584]{1,0:T(8,128)(2,1)S(1)}, bf16[8,2048]{1,0:T(8,128)(2,1)S(1)}, bf16[64,2048]{1,0:T(8,128)(2,1)S(1)}, bf16[64,3584]{1,0:T(8,128)(2,1)S...) custom-call(bf16[8,2048]{1,0:T(8,128)(2,1)S(1)} %copy-done.1, bf16[2048,3584]{1,0:T(8,128)(2,1)} %w_hbm.1, ...), custom_call_target="tpu_custom_call" | custom-call | flops 1879048192 | bytes 14680064 | tf_op jit(solution)/shard_map/exchange/pallas_call | solution.py:251
  28.6 5.4 %weight_grad.1 = (bf16[16,3584]{1,0:T(8,128)(2,1)}, bf16[8,2048]{1,0:T(8,128)(2,1)}, bf16[2048,3584]{1,0:T(8,128)(2,1)}) custom-call(bf16[64,2048]{1,0:T(8,128)(2,1)S(1)} %get-tuple-element.9.act_ref, bf16[64,3584]{1,0:T(8,128)(2,1)S(1)} %get-tuple-element.10.og_ref, f32[32,3584]{1,0:T(8,128)S(1)} %get-tuple-element.11.mask_ref, ...), custom_call_target="tpu_custom_call" | custom-call | flops 939524096 | bytes 14680064 | tf_op jit(solution)/shard_map/weight_grad/pallas_call | solution.py:287
Async XLA Ops:
  0.6 0.9 %copy-start = (bf16[16,3584]{1,0:T(8,128)(2,1)S(1)}, bf16[16,3584]{1,0:T(8,128)(2,1)}, u32[]{:S(2)}) copy-start(bf16[16,3584]{1,0:T(8,128)(2,1)} %og_hbm.1) | copy-start | bytes 344068
  1.5 0.8 %copy-start.1 = (bf16[8,2048]{1,0:T(8,128)(2,1)S(1)}, bf16[8,2048]{1,0:T(8,128)(2,1)}, u32[]{:S(2)}) copy-start(bf16[8,2048]{1,0:T(8,128)(2,1)} %act_hbm.1) | copy-start | bytes 98308
  2.3 0.7 %copy-start.2 = (s32[32,56]{1,0:T(8,128)S(1)}, s32[32,56]{1,0:T(8,128)}, u32[]{:S(2)}) copy-start(s32[32,56]{1,0:T(8,128)} %mask_hbm.1) | copy-start | bytes 21508

commit v3 on v2

--- a/solution.py
+++ b/solution.py
@@ -42,7 +42,7 @@
     nw, nn, side,
     act_hbm, w_hbm, mask_hbm, og_hbm,
     out_ref, ig_ref, act_out, og_out, mask_out, grad_out,
-    w, mask, act_all, og_all, ig_part, ig_recv, out_part, out_recv,
+    w, mask, act_all, og_all, og_turned, ig_part, ig_recv, out_part, out_recv,
     in_sem, w_sem, act_send, act_recv, og_send, og_recv,
     ig_send, ig_rsem, out_send, out_rsem,
 ):
@@ -127,11 +127,12 @@
             at = pl.ds(pl.multiple_of(c * ROWS + b * side, side), side)
             w[at, :] = w[at, :] * kept
 
-    pl.loop(0, steps // 2)(mask_rows)
+    ahead = steps - steps // 4
+    pl.loop(0, ahead)(mask_rows)
     for arrived, passed in zip(far, near[1:]):
         arrived.wait_recv()
         passed.start()
-    pl.loop(steps // 2, steps)(mask_rows)
+    pl.loop(ahead, steps)(mask_rows)
 
     for copy in far:
         copy.wait_send()
@@ -140,6 +141,7 @@
     for copy in own_copies[1:]:
         copy.wait()
     og_out[...] = og_all[...].reshape(tokens, cols)
+    og_turned[...] = og_out[...].T
 
     ig_copies = []
     for part, (start, stop) in enumerate(halves(steps)):
@@ -147,9 +149,7 @@
         @pl.loop(start, stop)
         def _(c):
             at = pl.ds(pl.multiple_of(c * ROWS, ROWS), ROWS)
-            term = lax.dot_general(
-                og_out[...], w[at, :], (((1,), (1,)), ((), ())), preferred_element_type=F32
-            )
+            term = jnp.dot(w[at, :], og_turned[...], preferred_element_type=F32).T
             ig_part[:, :, at] = term.reshape(nw, tokens // nw, ROWS).astype(BF16)
 
         at = pl.ds(start * ROWS, (stop - start) * ROWS)
@@ -265,6 +265,7 @@
             pltpu.VMEM(block_mask.shape, block_mask.dtype),
             pltpu.VMEM((nw, own_w, rows), BF16),
             pltpu.VMEM((nn, own_n, cols), BF16),
+            pltpu.VMEM((cols, tokens), BF16),
             pltpu.VMEM((nw, own_w, rows), BF16),
             pltpu.VMEM((nw, own_w, rows), BF16),
             pltpu.VMEM((nn, own_n, cols), BF16),

time: 34.2 us -> 34.6 us (1.012)
    pallas_call x1, Pallas kernels: 25.6 us -> 25.9 us  [on_device(): pl.pallas_call(functools.partial(exchange_kernel, nw, nn, side), out_shap...]
where the time goes in v3:
time: 34.6 us; the launch traced here: 34.3 us
  Pallas kernels  31.3 us (90%)
  local copies, waits for them, and re-layouts  2.37 us (7%)
  between operations  0.65 us (2%)
    pallas_call x1, Pallas kernels, on_device(): pl.pallas_call(functools.partial(exchange_kernel, nw, nn, side), out_shap...  25.9 us
    pallas_call x1, Pallas kernels, on_device(): pl.pallas_call(functools.partial(weight_kernel, side), out_shape=(shape((...  5.41 us
    unnamed x6, local copies, waits for them, and re-layouts  2.37 us

profile of v3, /device:TPU:1, one launch (start us, length us, event | category | flops | bytes accessed | tf_op | source)
XLA Modules:
  0.0 34.3 jit_solution(15531557370669313277)
XLA Ops:
  0.6 0.0 copy-start
  0.6 0.9 %copy-done = bf16[16,3584]{1,0:T(8,128)(2,1)S(1)} copy-done((bf16[16,3584]{1,0:T(8,128)(2,1)S(1)}, bf16[16,3584]{1,0:T(8,128)(2,1)}, u32[]{:S(2)}) %copy-start) | copy-done | bytes 114712
  1.5 0.0 copy-start.1
  1.5 0.8 %copy-done.1 = bf16[8,2048]{1,0:T(8,128)(2,1)S(1)} copy-done((bf16[8,2048]{1,0:T(8,128)(2,1)S(1)}, bf16[8,2048]{1,0:T(8,128)(2,1)}, u32[]{:S(2)}) %copy-start.1) | copy-done | bytes 32792
  2.3 0.0 copy-start.2
  2.3 0.7 %copy-done.2 = s32[32,56]{1,0:T(8,128)S(1)} copy-done((s32[32,56]{1,0:T(8,128)S(1)}, s32[32,56]{1,0:T(8,128)}, u32[]{:S(2)}) %copy-start.2) | copy-done | bytes 7192
  3.0 25.9 %exchange.1 = (bf16[16,3584]{1,0:T(8,128)(2,1)S(1)}, bf16[8,2048]{1,0:T(8,128)(2,1)S(1)}, bf16[64,2048]{1,0:T(8,128)(2,1)S(1)}, bf16[64,3584]{1,0:T(8,128)(2,1)S...) custom-call(bf16[8,2048]{1,0:T(8,128)(2,1)S(1)} %copy-done.1, bf16[2048,3584]{1,0:T(8,128)(2,1)} %w_hbm.1, ...), custom_call_target="tpu_custom_call" | custom-call | flops 1879048192 | bytes 14680064 | tf_op jit(solution)/shard_map/exchange/pallas_call | solution.py:251
  28.9 5.4 %weight_grad.1 = (bf16[16,3584]{1,0:T(8,128)(2,1)}, bf16[8,2048]{1,0:T(8,128)(2,1)}, bf16[2048,3584]{1,0:T(8,128)(2,1)}) custom-call(bf16[64,2048]{1,0:T(8,128)(2,1)S(1)} %get-tuple-element.9.act_ref, bf16[64,3584]{1,0:T(8,128)(2,1)S(1)} %get-tuple-element.10.og_ref, f32[32,3584]{1,0:T(8,128)S(1)} %get-tuple-element.11.mask_ref, ...), custom_call_target="tpu_custom_call" | custom-call | flops 939524096 | bytes 14680064 | tf_op jit(solution)/shard_map/weight_grad/pallas_call | solution.py:288
Async XLA Ops:
  0.6 0.9 %copy-start = (bf16[16,3584]{1,0:T(8,128)(2,1)S(1)}, bf16[16,3584]{1,0:T(8,128)(2,1)}, u32[]{:S(2)}) copy-start(bf16[16,3584]{1,0:T(8,128)(2,1)} %og_hbm.1) | copy-start | bytes 344068
  1.5 0.8 %copy-start.1 = (bf16[8,2048]{1,0:T(8,128)(2,1)S(1)}, bf16[8,2048]{1,0:T(8,128)(2,1)}, u32[]{:S(2)}) copy-start(bf16[8,2048]{1,0:T(8,128)(2,1)} %act_hbm.1) | copy-start | bytes 98308
  2.3 0.7 %copy-start.2 = (s32[32,56]{1,0:T(8,128)S(1)}, s32[32,56]{1,0:T(8,128)}, u32[]{:S(2)}) copy-start(s32[32,56]{1,0:T(8,128)} %mask_hbm.1) | copy-start | bytes 21508

commit v4 on v2

--- a/solution.py
+++ b/solution.py
@@ -25,7 +25,7 @@
 def grad_rows(side, act_ref, og_ref, mask_ref, first, grad_ref, at):
     cols = og_ref.shape[1]
     tile_cols = 256 if cols % 256 == 0 else cols
-    tile_rows = 2 * side
+    tile_rows = ROWS
     turned = act_ref[:, pl.ds(first, ROWS)].T
     for r in range(ROWS // tile_rows):
         left = turned[r * tile_rows:(r + 1) * tile_rows]

time: 34.2 us -> 34.2 us (level)
  no operation moved by 1% of the time
where the time goes in v4:
time: 34.2 us; the launch traced here: 34 us
  Pallas kernels  31 us (91%)
  local copies, waits for them, and re-layouts  2.37 us (7%)
  between operations  0.65 us (2%)
    pallas_call x1, Pallas kernels, on_device(): pl.pallas_call(functools.partial(exchange_kernel, nw, nn, side), out_shap...  25.6 us
    pallas_call x1, Pallas kernels, on_device(): pl.pallas_call(functools.partial(weight_kernel, side), out_shape=(shape((...  5.41 us
    unnamed x6, local copies, waits for them, and re-layouts  2.37 us

profile of v4, /device:TPU:1, one launch (start us, length us, event | category | flops | bytes accessed | tf_op | source)
XLA Modules:
  0.0 34.0 jit_solution(10058227722937216901)
XLA Ops:
  0.6 0.0 copy-start
  0.6 0.9 %copy-done = bf16[16,3584]{1,0:T(8,128)(2,1)S(1)} copy-done((bf16[16,3584]{1,0:T(8,128)(2,1)S(1)}, bf16[16,3584]{1,0:T(8,128)(2,1)}, u32[]{:S(2)}) %copy-start) | copy-done | bytes 114712
  1.5 0.0 copy-start.1
  1.5 0.8 %copy-done.1 = bf16[8,2048]{1,0:T(8,128)(2,1)S(1)} copy-done((bf16[8,2048]{1,0:T(8,128)(2,1)S(1)}, bf16[8,2048]{1,0:T(8,128)(2,1)}, u32[]{:S(2)}) %copy-start.1) | copy-done | bytes 32792
  2.3 0.0 copy-start.2
  2.3 0.7 %copy-done.2 = s32[32,56]{1,0:T(8,128)S(1)} copy-done((s32[32,56]{1,0:T(8,128)S(1)}, s32[32,56]{1,0:T(8,128)}, u32[]{:S(2)}) %copy-start.2) | copy-done | bytes 7192
  3.0 25.6 %exchange.1 = (bf16[16,3584]{1,0:T(8,128)(2,1)S(1)}, bf16[8,2048]{1,0:T(8,128)(2,1)S(1)}, bf16[64,2048]{1,0:T(8,128)(2,1)S(1)}, bf16[64,3584]{1,0:T(8,128)(2,1)S...) custom-call(bf16[8,2048]{1,0:T(8,128)(2,1)S(1)} %copy-done.1, bf16[2048,3584]{1,0:T(8,128)(2,1)} %w_hbm.1, ...), custom_call_target="tpu_custom_call" | custom-call | flops 1879048192 | bytes 14680064 | tf_op jit(solution)/shard_map/exchange/pallas_call | solution.py:251
  28.6 5.4 %weight_grad.1 = (bf16[16,3584]{1,0:T(8,128)(2,1)}, bf16[8,2048]{1,0:T(8,128)(2,1)}, bf16[2048,3584]{1,0:T(8,128)(2,1)}) custom-call(bf16[64,2048]{1,0:T(8,128)(2,1)S(1)} %get-tuple-element.9.act_ref, bf16[64,3584]{1,0:T(8,128)(2,1)S(1)} %get-tuple-element.10.og_ref, f32[32,3584]{1,0:T(8,128)S(1)} %get-tuple-element.11.mask_ref, ...), custom_call_target="tpu_custom_call" | custom-call | flops 939524096 | bytes 14680064 | tf_op jit(solution)/shard_map/weight_grad/pallas_call | solution.py:287
Async XLA Ops:
  0.6 0.9 %copy-start = (bf16[16,3584]{1,0:T(8,128)(2,1)S(1)}, bf16[16,3584]{1,0:T(8,128)(2,1)}, u32[]{:S(2)}) copy-start(bf16[16,3584]{1,0:T(8,128)(2,1)} %og_hbm.1) | copy-start | bytes 344068
  1.5 0.8 %copy-start.1 = (bf16[8,2048]{1,0:T(8,128)(2,1)S(1)}, bf16[8,2048]{1,0:T(8,128)(2,1)}, u32[]{:S(2)}) copy-start(bf16[8,2048]{1,0:T(8,128)(2,1)} %act_hbm.1) | copy-start | bytes 98308
  2.3 0.7 %copy-start.2 = (s32[32,56]{1,0:T(8,128)S(1)}, s32[32,56]{1,0:T(8,128)}, u32[]{:S(2)}) copy-start(s32[32,56]{1,0:T(8,128)} %mask_hbm.1) | copy-start | bytes 21508
